TPU v7x, 32 devices: a whole 2x2x4 slice. The times are simulated.
32 devices in a mesh: dp: 16 (over z, y, core), tensor: 2 (over x).
Axes of the slice: x: 2, y: 2, z: 4, core: 2. Of those that a mesh axis runs over, the one named last changes fastest.
Arguments:
- inputs: bfloat16 [32, 512, 768], P('dp'), may hold values from -6 to 6
- lengths: int32 [32], P('dp'), may hold values from 16 to 512, as said below
- w_query: bfloat16 [768, 768], P(None, 'tensor'), may hold values from -0.21875 to 0.21875
- b_query: bfloat16 [768], P('tensor'), may hold values from -3 to 3
- w_key: bfloat16 [768, 768], P(None, 'tensor'), may hold values from -0.21875 to 0.21875
- w_value: bfloat16 [768, 768], P(None, 'tensor'), may hold values from -0.21875 to 0.21875
- b_value: bfloat16 [768], P('tensor'), may hold values from -3 to 3
- w_output: bfloat16 [768, 768], P('tensor'), may hold values from -0.875 to 0.875
- b_output: bfloat16 [768], replicated, may hold values from -3 to 3
- gain_one: bfloat16 [768], replicated, may hold values from 0.5 to 1.5
- shift_one: bfloat16 [768], replicated, may hold values from -3 to 3
- w_up: bfloat16 [768, 3072], P(None, 'tensor'), may hold values from -0.21875 to 0.21875
- b_up: bfloat16 [3072], P('tensor'), may hold values from -3 to 3
- w_down: bfloat16 [3072, 768], P('tensor'), may hold values from -0.109375 to 0.109375
- b_down: bfloat16 [768], replicated, may hold values from -3 to 3
- gain_two: bfloat16 [768], replicated, may hold values from 0.5 to 1.5
- shift_two: bfloat16 [768], replicated, may hold values from -3 to 3
- cotangent: bfloat16 [32, 512, 768], P('dp'), may hold values from -6 to 6
Outputs:
- layer_out: bfloat16 [32, 512, 768], P('dp')
- grad_inputs: bfloat16 [32, 512, 768], P('dp')
- grad_w_query: float32 [768, 768], P('dp', 'tensor')
- grad_b_query: float32 [768], P('tensor')
- grad_w_key: float32 [768, 768], P('dp', 'tensor')
- grad_w_value: float32 [768, 768], P('dp', 'tensor')
- grad_b_value: float32 [768], P('tensor')
- grad_w_output: float32 [768, 768], P('tensor', 'dp')
- grad_b_output: float32 [768], P('dp')
- grad_gain_one: float32 [768], P('dp')
- grad_shift_one: float32 [768], P('dp')
- grad_w_up: float32 [768, 3072], P('dp', 'tensor')
- grad_b_up: float32 [3072], P('tensor')
- grad_w_down: float32 [3072, 768], P('tensor', 'dp')
- grad_b_down: float32 [768], P('dp')
- grad_gain_two: float32 [768], P('dp')
- grad_shift_two: float32 [768], P('dp')
Inputs may be any that keep to these rules, and one draw needn't show every extreme that they name: `lengths`: positions at or past a sentence's length are padding; some sentence has length 512 in every draw.
All inputs are finite; a program needn't handle non-finite values.
Results may differ from a plain program's by a relative error of at most 0.013.
Values sent between devices are 32-bit elements; how exact they have to be, the bound alone decides.
No kernel may reach another device: no remote copies, remote signals or barrier semaphores. Data moves between devices by JAX's collectives and lax.ppermute only.
A program may use at most 128 MiB of HBM per device.

v0:
```python
import jax
import jax.numpy as jnp
from jax import lax
from jax.sharding import PartitionSpec as P

DH = 64


norm_eps = 1e-12
masked_score = -1000000000.0


def over_rows(left, right):
    return lax.dot_general(
        left, right, (((0,), (0,)), ((), ())), preferred_element_type=jnp.float32
    )


def against(left, right):
    return lax.dot_general(
        left, right, (((1,), (1,)), ((), ())), preferred_element_type=jnp.float32
    )


def norm_forward(values, gain, shift):
    center = values - jnp.mean(values, axis=-1, keepdims=True)
    spread = jnp.mean(center * center, axis=-1, keepdims=True)
    inverse = lax.rsqrt(spread + norm_eps)
    normed = center * inverse
    return (normed * gain + shift, normed, inverse)


def norm_backward(grad, normed, inverse, gain):
    scaled = grad * gain
    mean_one = jnp.mean(scaled, axis=-1, keepdims=True)
    mean_two = jnp.mean(scaled * normed, axis=-1, keepdims=True)
    return inverse * (scaled - mean_one - normed * mean_two)


def exact_gelu(value):
    return jax.nn.gelu(value, approximate=False)


def per_device(
    inputs,
    lengths,
    w_query,
    b_query,
    w_key,
    w_value,
    b_value,
    w_output,
    b_output,
    gain_one,
    shift_one,
    w_up,
    b_up,
    w_down,
    b_down,
    gain_two,
    shift_two,
    cotangent,
):
    count, length, width = inputs.shape
    heads = w_query.shape[1] // DH
    local_width = heads * DH
    flat = inputs.reshape(count * length, width)
    positions = jnp.arange(length, dtype=jnp.int32)
    valid = positions[None, :] < lengths[:, None]
    gain_first = gain_one.astype(jnp.float32)
    gain_second = gain_two.astype(jnp.float32)
    query = (
        jnp.dot(flat, w_query, preferred_element_type=jnp.float32) + b_query.astype(jnp.float32)
    ).astype(jnp.bfloat16)
    keys = jnp.dot(flat, w_key, preferred_element_type=jnp.float32).astype(jnp.bfloat16)
    values = (
        jnp.dot(flat, w_value, preferred_element_type=jnp.float32) + b_value.astype(jnp.float32)
    ).astype(jnp.bfloat16)
    query = query.reshape(count, length, heads, DH)
    keys = keys.reshape(count, length, heads, DH)
    values = values.reshape(count, length, heads, DH)
    scores = jnp.einsum("sqhd,skhd->shqk", query, keys, preferred_element_type=jnp.float32) * 0.125
    scores = jnp.where(valid[:, None, None, :], scores, masked_score)
    top = jnp.max(scores, axis=-1, keepdims=True)
    expo = jnp.exp(scores - top)
    total = jnp.sum(expo, axis=-1, keepdims=True)
    probs_low = (expo / total).astype(jnp.bfloat16)
    log_total = top + jnp.log(total)
    context = jnp.einsum("shqk,skhd->sqhd", probs_low, values, preferred_element_type=jnp.float32)
    context = context.astype(jnp.bfloat16).reshape(count * length, local_width)
    attn = lax.psum(jnp.dot(context, w_output, preferred_element_type=jnp.float32), "tensor")
    residual_one = flat.astype(jnp.float32) + attn + b_output.astype(jnp.float32)
    first, normed_one, inverse_one = norm_forward(
        residual_one, gain_first, shift_one.astype(jnp.float32)
    )
    first_low = first.astype(jnp.bfloat16)
    pre = jnp.dot(first_low, w_up, preferred_element_type=jnp.float32) + b_up.astype(jnp.float32)
    act_full, gelu_back = jax.vjp(exact_gelu, pre)
    act = act_full.astype(jnp.bfloat16)
    ffn = lax.psum(jnp.dot(act, w_down, preferred_element_type=jnp.float32), "tensor")
    residual_two = first + ffn + b_down.astype(jnp.float32)
    final, normed_two, inverse_two = norm_forward(
        residual_two, gain_second, shift_two.astype(jnp.float32)
    )
    layer_out = final.astype(jnp.bfloat16).reshape(count, length, width)
    tangent = cotangent.reshape(count * length, width).astype(jnp.float32)
    grad_gain_two = jnp.sum(tangent * normed_two, axis=0)
    grad_shift_two = jnp.sum(tangent, axis=0)
    d_second = norm_backward(tangent, normed_two, inverse_two, gain_second)
    d_ffn = d_second.astype(jnp.bfloat16)
    grad_b_down = jnp.sum(d_second, axis=0)
    grad_w_down = over_rows(act, d_ffn)
    d_pre = gelu_back(against(d_ffn, w_down))[0].astype(jnp.bfloat16)
    grad_b_up = jnp.sum(d_pre.astype(jnp.float32), axis=0)
    grad_w_up = over_rows(first_low, d_pre)
    d_first = d_second + lax.psum(against(d_pre, w_up), "tensor")
    grad_gain_one = jnp.sum(d_first * normed_one, axis=0)
    grad_shift_one = jnp.sum(d_first, axis=0)
    d_res_one = norm_backward(d_first, normed_one, inverse_one, gain_first)
    d_attn = d_res_one.astype(jnp.bfloat16)
    grad_b_output = jnp.sum(d_res_one, axis=0)
    grad_w_output = over_rows(context, d_attn)
    d_context = against(d_attn, w_output).astype(jnp.bfloat16).reshape(count, length, heads, DH)
    again = jnp.einsum("sqhd,skhd->shqk", query, keys, preferred_element_type=jnp.float32) * 0.125
    again = jnp.where(valid[:, None, None, :], again, masked_score)
    probs = jnp.exp(again - log_total)
    probs_again = probs.astype(jnp.bfloat16)
    d_value = jnp.einsum(
        "shqk,sqhd->skhd", probs_again, d_context, preferred_element_type=jnp.float32
    ).astype(jnp.bfloat16)
    d_probs = jnp.einsum("sqhd,skhd->shqk", d_context, values, preferred_element_type=jnp.float32)
    d_scores = probs * (d_probs - jnp.sum(probs * d_probs, axis=-1, keepdims=True))
    d_scores = d_scores.astype(jnp.bfloat16)
    d_query = (
        jnp.einsum("shqk,skhd->sqhd", d_scores, keys, preferred_element_type=jnp.float32) * 0.125
    ).astype(jnp.bfloat16)
    d_key = (
        jnp.einsum("shqk,sqhd->skhd", d_scores, query, preferred_element_type=jnp.float32) * 0.125
    ).astype(jnp.bfloat16)
    d_query = d_query.reshape(count * length, local_width)
    d_key = d_key.reshape(count * length, local_width)
    d_value = d_value.reshape(count * length, local_width)
    grad_b_query = jnp.sum(d_query.astype(jnp.float32), axis=0)
    grad_b_value = jnp.sum(d_value.astype(jnp.float32), axis=0)
    grad_w_query = over_rows(flat, d_query)
    grad_w_key = over_rows(flat, d_key)
    grad_w_value = over_rows(flat, d_value)
    through = against(d_query, w_query) + against(d_key, w_key) + against(d_value, w_value)
    d_inputs = d_res_one + lax.psum(through, "tensor")
    grad_inputs = d_inputs.astype(jnp.bfloat16).reshape(count, length, width)
    (
        summed_query,
        summed_key,
        summed_value,
        summed_output,
        summed_up,
        summed_down,
        summed_bias_output,
        summed_bias_down,
        summed_gain_one,
        summed_shift_one,
        summed_gain_two,
        summed_shift_two,
    ) = (
        lax.psum_scatter(grad_w_query, "dp", scatter_dimension=0, tiled=True),
        lax.psum_scatter(grad_w_key, "dp", scatter_dimension=0, tiled=True),
        lax.psum_scatter(grad_w_value, "dp", scatter_dimension=0, tiled=True),
        lax.psum_scatter(grad_w_output, "dp", scatter_dimension=1, tiled=True),
        lax.psum_scatter(grad_w_up, "dp", scatter_dimension=0, tiled=True),
        lax.psum_scatter(grad_w_down, "dp", scatter_dimension=1, tiled=True),
        lax.psum_scatter(grad_b_output, "dp", scatter_dimension=0, tiled=True),
        lax.psum_scatter(grad_b_down, "dp", scatter_dimension=0, tiled=True),
        lax.psum_scatter(grad_gain_one, "dp", scatter_dimension=0, tiled=True),
        lax.psum_scatter(grad_shift_one, "dp", scatter_dimension=0, tiled=True),
        lax.psum_scatter(grad_gain_two, "dp", scatter_dimension=0, tiled=True),
        lax.psum_scatter(grad_shift_two, "dp", scatter_dimension=0, tiled=True),
    )
    summed_bias_query, summed_bias_value, summed_bias_up = lax.psum(
        (grad_b_query, grad_b_value, grad_b_up), "dp"
    )
    return (
        layer_out,
        grad_inputs,
        summed_query,
        summed_bias_query,
        summed_key,
        summed_value,
        summed_bias_value,
        summed_output,
        summed_bias_output,
        summed_gain_one,
        summed_shift_one,
        summed_up,
        summed_bias_up,
        summed_down,
        summed_bias_down,
        summed_gain_two,
        summed_shift_two,
    )


def solution(mesh):
    in_specs = (
        P("dp", None, None),
        P("dp"),
        P(None, "tensor"),
        P("tensor"),
        P(None, "tensor"),
        P(None, "tensor"),
        P("tensor"),
        P("tensor", None),
        P(),
        P(),
        P(),
        P(None, "tensor"),
        P("tensor"),
        P("tensor", None),
        P(),
        P(),
        P(),
        P("dp", None, None),
    )
    out_specs = (
        P("dp", None, None),
        P("dp", None, None),
        P("dp", "tensor"),
        P("tensor"),
        P("dp", "tensor"),
        P("dp", "tensor"),
        P("tensor"),
        P("tensor", "dp"),
        P("dp"),
        P("dp"),
        P("dp"),
        P("dp", "tensor"),
        P("tensor"),
        P("tensor", "dp"),
        P("dp"),
        P("dp"),
        P("dp"),
    )
    return jax.shard_map(
        per_device, mesh=mesh, in_specs=in_specs, out_specs=out_specs, check_vma=False
    )
```

profile of v0, /device:TPU:0, one launch (start us, length us, event | category | flops | bytes accessed | tf_op | source)
XLA Modules:
  0.0 908.1 jit_solution(16803506148612957902)
XLA Ops:
  28.3 4.5 fusion.12
  45.1 88.0 %all-reduce.12.cloned.1.call-done = f32[1024,768]{1,0:T(8,128)} async-done(((f32[1024,768]{1,0:T(8,128)}), f32[1024,768]{1,0:T(8,128)}) %all-reduce.12.cloned.1.call-update) | async-done | bytes 3145744 | tf_op jit(solution)/shard_map/psum | solution.py:91
  136.5 17.6 %multiply_convert_fusion.1 = (bf16[1024,1536]{1,0:T(8,128)(2,1)S(1)}, f32[1024,1536]{1,0:T(8,128)}, f32[1024,1536]{1,0:T(8,128)}) fusion(f32[1536]{0:T(1024)S(1)} %convert_element_type.130, bf16[768,1536]{1,0:T(8,128)(2,1)S(1)} %copy-done, f32[1024,768]{1,0:T(8,128)S(1)} %get-tuple-element.95, f32[768]{0:T(1024)S(1)} %convert_element_type.128, ...), kind=kOutput, calls=%fused_computation.14 | convolution fusion | flops 2523660288 | bytes 21254144 | tf_op jit(solution)/shard_map/dot_general | solution.py:97
  155.8 4.3 fusion.65
  163.6 82.5 %all-reduce.14.cloned.1.call-done = f32[1024,768]{1,0:T(8,128)} async-done(((f32[1024,768]{1,0:T(8,128)}), f32[1024,768]{1,0:T(8,128)}) %all-reduce.14.cloned.1.call-update) | async-done | bytes 3145744 | tf_op jit(solution)/shard_map/psum | solution.py:100
  246.1 4.0 fusion.61
  255.7 8.4 convert_reduce_fusion
  265.7 4.3 fusion.66
  270.3 85.7 %all-reduce.16.cloned.1.call-done = f32[1024,768]{1,0:T(8,128)} async-done(((f32[1024,768]{1,0:T(8,128)}), f32[1024,768]{1,0:T(8,128)}) %all-reduce.16.cloned.1.call-update) | async-done | bytes 3145744 | tf_op jit(solution)/shard_map/psum | solution.py:116
  356.0 5.4 multiply_reduce_fusion.1
  372.2 9.5 %convert_reduce_fusion.2 = (f32[6,64]{1,0:T(8,128)}, bf16[2,512,6,64]{1,3,2,0:T(8,128)(2,1)}) fusion(f32[2,6,512]{2,1,0:T(8,128)S(1)} %log_add_fusion, f32[2,6,512,512]{2,3,1,0:T(8,128)} %copy-done.1, pred[2,512]{1,0:T(4,128)(4,1)S(1)} %iota_compare_fusion, bf16[2,512,6,64]{1,0,3,2:T(2,128)(2,1)} %reshape.165), kind=kOutput, calls=%fused_computation.56 | convolution fusion | flops 416415360 | bytes 14182912 | tf_op jit(solution)/shard_map/shqk,sqhd->skhd/dot_general | solution.py:128
  381.7 9.7 %multiply_reduce_fusion = (f32[2,6,512]{2,1,0:T(8,128)S(1)}, f32[2,6,512,512]{2,3,1,0:T(8,128)}) fusion(f32[2,6,512]{2,1,0:T(8,128)S(1)} %log_add_fusion, f32[2,6,512,512]{2,3,1,0:T(8,128)} %copy-done.1, pred[2,512]{1,0:T(4,128)(4,1)S(1)} %iota_compare_fusion, bf16[2,512,6,64]{1,0,3,2:T(2,128)(2,1)S(1)} %copy-done.11, bf16[2,512,6,64]{1,0,3,2:T(2,128)(2,1)S(1)} %copy-done.12), kind=kOutput, calls=%fused_computation.1 | convolution fusion | flops 418375680 | bytes 26788864 | tf_op jit(solution)/shard_map/sqhd,skhd->shqk/dot_general | solution.py:131
  391.4 7.6 multiply_convert_fusion
  410.6 3.9 fusion.31
  431.3 7.6 fusion.34
  439.6 8.0 fusion.54
  449.6 60.9 %all-reduce.6 = (f32[384]{0:T(512)}, f32[384]{0:T(512)}, f32[768]{0:T(1024)S(1)}, f32[768]{0:T(1024)S(1)}, f32[768]{0:T(1024)S(1)}, /*index=5*/f32[1536]{0:T(102...) all-reduce(f32[384]{0:T(512)S(1)} %reduce_sum.186, ...), channel_id=1, replica_groups=mesh['dp'=16,'tensor'=2] {'dp'}, use_global_device_ids=true, to_apply=%region_17.18 | all-reduce | flops 6912 | bytes 55296 | tf_op jit(solution)/shard_map/psum | solution.py:178
  514.1 4.4 add_convert_fusion.1
  518.4 40.2 %reduce-scatter.13.cloned.1.call-done = f32[384,48]{0,1:T(8,128)} async-done(((f32[384,768]{0,1:T(8,128)}), f32[384,48]{0,1:T(8,128)}) %reduce-scatter.13.cloned.1.call-update) | async-done | bytes 73744 | tf_op jit(solution)/shard_map/reduce_scatter | solution.py:168
  558.6 61.1 %reduce-scatter.23.cloned.1.call-done = f32[48,384]{1,0:T(8,128)} async-done(((f32[768,384]{1,0:T(8,128)}), f32[48,384]{1,0:T(8,128)}) %reduce-scatter.23.cloned.1.call-update) | async-done | bytes 73744
  619.7 61.3 %reduce-scatter.19.cloned.1.call-done = f32[48,384]{1,0:T(8,128)} async-done(((f32[768,384]{1,0:T(8,128)}), f32[48,384]{1,0:T(8,128)}) %reduce-scatter.19.cloned.1.call-update) | async-done | bytes 73744
  681.0 61.4 %reduce-scatter.21.cloned.1.call-done = f32[48,384]{1,0:T(8,128)} async-done(((f32[768,384]{1,0:T(8,128)}), f32[48,384]{1,0:T(8,128)}) %reduce-scatter.21.cloned.1.call-update) | async-done | bytes 73744
  742.4 79.1 %reduce-scatter.17.cloned.1.call-done = f32[1536,48]{0,1:T(8,128)} async-done(((f32[1536,768]{0,1:T(8,128)}), f32[1536,48]{0,1:T(8,128)}) %reduce-scatter.17.cloned.1.call-update) | async-done | bytes 294928 | tf_op jit(solution)/shard_map/reduce_scatter | solution.py:170
  821.4 79.4 %reduce-scatter.15.cloned.1.call-done = f32[48,1536]{1,0:T(8,128)} async-done(((f32[768,1536]{1,0:T(8,128)}), f32[48,1536]{1,0:T(8,128)}) %reduce-scatter.15.cloned.1.call-update) | async-done | bytes 294928 | tf_op jit(solution)/shard_map/reduce_scatter | solution.py:169
  (192 shorter events, 93.4 us)
Async XLA Ops:
  7.2 129.3 %copy-start = (bf16[768,1536]{1,0:T(8,128)(2,1)S(1)}, bf16[768,1536]{1,0:T(8,128)(2,1)}, u32[]{:S(2)}) copy-start(bf16[768,1536]{1,0:T(8,128)(2,1)} %param.29) | copy-start | bytes 7077892
  7.2 125.9 %all-reduce.12.cloned.1.call-start = ((), (), s32[]{:S(2)}) async-start(), calls=%async_computation.6 | async-start | bytes 6291456 | tf_op jit(solution)/shard_map/psum | solution.py:91
  44.5 201.6 %all-reduce.14.cloned.1.call-start = ((), (), s32[]{:S(2)}) async-start(), calls=%async_computation.7 | async-start | bytes 6291456 | tf_op jit(solution)/shard_map/psum | solution.py:100
  45.0 201.1 %copy-start.28 = (f32[768]{0:T(1024)}, f32[768]{0:T(1024)S(1)}, u32[]{:S(2)}) copy-start(f32[768]{0:T(1024)S(1)} %convert_element_type.128) | copy-start | bytes 9220
  135.9 18.1 %copy-start.2 = (f32[1024,768]{1,0:T(8,128)}, f32[1024,768]{1,0:T(8,128)S(1)}, u32[]{:S(2)}) copy-start(f32[1024,768]{1,0:T(8,128)S(1)} %get-tuple-element.95) | copy-start | bytes 9437188
  136.5 19.3 %copy-start.40 = (bf16[1536,768]{1,0:T(8,128)(2,1)S(1)}, bf16[1536,768]{1,0:T(8,128)(2,1)}, u32[]{:S(2)}) copy-start(bf16[1536,768]{1,0:T(8,128)(2,1)} %param.31) | copy-start | bytes 7077892
  160.2 195.8 %all-reduce.16.cloned.1.call-start = ((), (), s32[]{:S(2)}) async-start(), calls=%async_computation.8 | async-start | bytes 6291456 | tf_op jit(solution)/shard_map/psum | solution.py:116
  246.1 9.5 %slice-start.3 = ((s8[6291456]{0:T(1024)(128)(4,1)}), s8[4194304]{0:T(1024)(128)(4,1)S(1)}, s32[]{:S(2)}) async-start(s8[6291456]{0:T(1024)(128)(4,1)} %bitcast.125), calls=%async_computation.19 | async-start | bytes 8388608
  255.6 8.5 copy-start.6
  270.0 244.0 %all-reduce.18.cloned.1.call-start = ((), (), s32[]{:S(2)}) async-start(), calls=%async_computation.9 | async-start | bytes 6291456 | tf_op jit(solution)/shard_map/psum | solution.py:149
  356.0 5.4 copy-start.3
  372.2 9.5 %copy-start.11 = (bf16[2,512,6,64]{1,0,3,2:T(2,128)(2,1)S(1)}, bf16[2,512,6,64]{1,0,3,2:T(2,128)(2,1)}, u32[]{:S(2)}) copy-start(bf16[2,512,6,64]{1,0,3,2:T(2,128)(2,1)} %reshape.160) | copy-start | bytes 2359300
  372.2 9.5 %copy-start.12 = (bf16[2,512,6,64]{1,0,3,2:T(2,128)(2,1)S(1)}, bf16[2,512,6,64]{1,0,3,2:T(2,128)(2,1)}, u32[]{:S(2)}) copy-start(bf16[2,512,6,64]{1,0,3,2:T(2,128)(2,1)} %reshape.165) | copy-start | bytes 2359300
  372.2 19.1 %slice-start = ((s8[12582912]{0:T(1024)(128)(4,1)}), s8[4194304]{0:T(1024)(128)(4,1)S(1)}, s32[]{:S(2)}) async-start(s8[12582912]{0:T(1024)(128)(4,1)} %bitcast.102), calls=%async_computation.16 | async-start | bytes 8388608
  372.2 19.1 %slice-start.1 = ((s8[12582912]{0:T(1024)(128)(4,1)}), s8[4194304]{0:T(1024)(128)(4,1)S(1)}, s32[]{:S(2)}) async-start(s8[12582912]{0:T(1024)(128)(4,1)} %bitcast.102), calls=%async_computation.17 | async-start | bytes 8388608
  381.7 9.7 %slice-start.2 = ((s8[12582912]{0:T(1024)(128)(4,1)}), s8[4194304]{0:T(1024)(128)(4,1)S(1)}, s32[]{:S(2)}) async-start(s8[12582912]{0:T(1024)(128)(4,1)} %bitcast.102), calls=%async_computation.18 | async-start | bytes 8388608
  391.3 7.6 copy-start.9
  410.5 148.1 %reduce-scatter.13.cloned.1.call-start = ((), (), s32[]{:S(2)}) async-start(), calls=%async_computation.10 | async-start | bytes 1253376 | tf_op jit(solution)/shard_map/reduce_scatter | solution.py:168
  414.6 205.2 %reduce-scatter.23.cloned.1.call-start = ((), (), s32[]{:S(2)}) async-start(), calls=%async_computation.15 | async-start | bytes 1253376
  418.8 6.3 copy-start.14
  418.8 262.3 %reduce-scatter.19.cloned.1.call-start = ((), (), s32[]{:S(2)}) async-start(), calls=%async_computation.13 | async-start | bytes 1253376
  425.0 317.4 %reduce-scatter.21.cloned.1.call-start = ((), (), s32[]{:S(2)}) async-start(), calls=%async_computation.14 | async-start | bytes 1253376
  431.0 390.5 %reduce-scatter.17.cloned.1.call-start = ((), (), s32[]{:S(2)}) async-start(), calls=%async_computation.12 | async-start | bytes 5013504 | tf_op jit(solution)/shard_map/reduce_scatter | solution.py:170
  438.9 461.9 %reduce-scatter.15.cloned.1.call-start = ((), (), s32[]{:S(2)}) async-start(), calls=%async_computation.11 | async-start | bytes 5013504 | tf_op jit(solution)/shard_map/reduce_scatter | solution.py:169
  (36 other events, 79.6 us)
Sparse Core Ops, SparseCore 0:
  44.6 88.4 all-reduce.11
  160.3 85.7 all-reduce.13
  270.1 85.7 all-reduce.15
  410.7 85.7 all-reduce.17
  500.5 58.0 reduce-scatter.12
  562.6 57.0 reduce-scatter.22
  623.9 57.0 reduce-scatter.18
  685.2 57.1 reduce-scatter.20
  746.8 74.5 reduce-scatter.16
  826.2 74.5 reduce-scatter.14
where the time goes:
time: 918 us; the launch traced here: 908 us
  waiting for transfers between devices  639 us (70%)
  matrix products  113 us (12%)
  blocking collectives  60.9 us (7%)
  other arithmetic  39.3 us (4%)
  local copies, waits for them, and re-layouts  38.9 us (4%)
  between operations  15.9 us (2%)
    unnamed x13, waiting for transfers between devices  184 us
    psum x1, waiting for transfers between devices, per_device(): lax.psum(jnp.dot(context, w_output, preferred_element_type=jnp.float32),...  88 us
    psum x1, waiting for transfers between devices, per_device(): d_first = d_second + lax.psum(against(d_pre, w_up), 'tensor')  85.7 us
    psum x1, waiting for transfers between devices, per_device(): lax.psum(jnp.dot(act, w_down, preferred_element_type=jnp.float32), 'tensor')  82.5 us
    reduce_scatter x1, waiting for transfers between devices, per_device(): lax.psum_scatter(grad_w_up, 'dp', scatter_dimension=0, tiled=True)  79.4 us
    reduce_scatter x1, waiting for transfers between devices, per_device(): lax.psum_scatter(grad_w_down, 'dp', scatter_dimension=1, tiled=True)  79.1 us
    psum x1, blocking collectives, per_device(): lax.psum((grad_b_query, grad_b_value, grad_b_up), 'dp')  60.9 us
    reduce_scatter x1, waiting for transfers between devices, per_device(): lax.psum_scatter(grad_w_output, 'dp', scatter_dimension=1, tiled=True)  40.2 us
  transfers between devices with their start and end apart: 10, of which 9 were waited for; matrix products, arithmetic and copies ran while one was open for 5% of the time, Pallas kernels for 0%

commit v1 on v0

v1 whole, which is shorter than its diff:
```python
import functools
import math

import jax
import jax.numpy as jnp
from jax import lax
from jax.experimental import pallas as pl
from jax.experimental.pallas import tpu as pltpu
from jax.sharding import PartitionSpec as P

DH = 64
PAIR = 2 * DH

norm_eps = 1e-12
masked_score = -1000000000.0
PARAMS = pltpu.CompilerParams(vmem_limit_bytes=48 * 1024 * 1024)


def over_rows(left, right):
    return lax.dot_general(
        left, right, (((0,), (0,)), ((), ())), preferred_element_type=jnp.float32
    )


def against(left, right):
    return lax.dot_general(
        left, right, (((1,), (1,)), ((), ())), preferred_element_type=jnp.float32
    )


def plain(left, right):
    return jnp.dot(left, right, preferred_element_type=jnp.float32)


def norm_forward(values, gain, shift):
    center = values - jnp.mean(values, axis=-1, keepdims=True)
    spread = jnp.mean(center * center, axis=-1, keepdims=True)
    inverse = lax.rsqrt(spread + norm_eps)
    normed = center * inverse
    return (normed * gain + shift, normed, inverse)


def norm_backward(grad, normed, inverse, gain):
    scaled = grad * gain
    mean_one = jnp.mean(scaled, axis=-1, keepdims=True)
    mean_two = jnp.mean(scaled * normed, axis=-1, keepdims=True)
    return inverse * (scaled - mean_one - normed * mean_two)


def gelu_both(value):
    phi_big = 0.5 + 0.5 * lax.erf(value * math.sqrt(0.5))
    phi_small = jnp.exp(-0.5 * value * value) * (1.0 / math.sqrt(2.0 * math.pi))
    return (value * phi_big).astype(jnp.bfloat16), (phi_big + value * phi_small).astype(jnp.bfloat16)


def swap_x(value):
    return lax.ppermute(value, "tensor", [(0, 1), (1, 0)])


def swap_dp(value, bit, n):
    return lax.ppermute(value, "dp", [(i, i ^ bit) for i in range(n)])


def place_kernel(slots, me_ref, *refs):
    out = refs[-1]
    rows = refs[0].shape[0]
    for slot, piece in zip(slots, refs[:-1]):
        at = jnp.bitwise_xor(jnp.bitwise_and(me_ref[0], 7), slot) * rows
        out[pl.ds(pl.multiple_of(at, rows), rows), :] = piece[...].astype(out.dtype)


def fetch_other(own, me, n, first, second):
    rows = own.shape[0] // 8
    mine = lax.dynamic_slice_in_dim(own, jnp.bitwise_and(me, 7) * rows, rows, 0)
    a = swap_x(mine.astype(jnp.float32))
    b = swap_dp(a, first, n)
    c, d = swap_dp(a, second, n), swap_dp(b, second, n)
    pieces = [a, b, c, d] + [swap_dp(v, 1, n) for v in (a, b, c, d)]
    slots = [0, first, second, first | second]
    slots = slots + [s | 1 for s in slots]
    return pl.pallas_call(
        functools.partial(place_kernel, slots),
        out_shape=jax.ShapeDtypeStruct(own.shape, own.dtype),
        in_specs=[pl.BlockSpec(memory_space=pltpu.SMEM)]
        + [pl.BlockSpec(memory_space=pltpu.VMEM)] * 8,
        out_specs=pl.BlockSpec(memory_space=pltpu.VMEM),
        compiler_params=PARAMS,
    )(me.reshape(1), *pieces)


def relative_chunks(n, order):
    steps = len(order)
    return [
        sum(bit for j, bit in enumerate(order) if (r >> (steps - 1 - j)) & 1) for r in range(n)
    ]


def turn_kernel(chunks, me_ref, x_ref, out_ref, scratch):
    rows = out_ref.shape[0] // len(chunks)
    scratch[...] = x_ref[...].T
    for r, chunk in enumerate(chunks):
        at = pl.multiple_of(jnp.bitwise_xor(me_ref[0], chunk) * rows, rows)
        out_ref[r * rows : (r + 1) * rows, :] = scratch[pl.ds(at, rows), :]


def turned(x, me, n, order):
    chunks = relative_chunks(n, order)
    rows = x.shape[1] // n
    if rows % 16:
        wanted = jnp.bitwise_xor(me, jnp.array(chunks, jnp.int32))
        return x.T.reshape(n, rows, x.shape[0])[wanted].reshape(x.shape[1], x.shape[0])
    return pl.pallas_call(
        functools.partial(turn_kernel, chunks),
        out_shape=jax.ShapeDtypeStruct((x.shape[1], x.shape[0]), x.dtype),
        in_specs=[
            pl.BlockSpec(memory_space=pltpu.SMEM),
            pl.BlockSpec(memory_space=pltpu.VMEM),
        ],
        out_specs=pl.BlockSpec(memory_space=pltpu.VMEM),
        scratch_shapes=[pltpu.VMEM((x.shape[1], x.shape[0]), x.dtype)],
        compiler_params=PARAMS,
    )(me.reshape(1), x)


def scatter_sum(grad, n, order):
    for bit in order:
        half = grad.shape[0] // 2
        grad = grad[:half] + swap_dp(grad[half:], bit, n)
    return grad


def total_sum(value, n, order):
    for bit in order:
        value = value + swap_dp(value, bit, n)
    return value


def attend_kernel(len_ref, x_ref, ctx_ref, lse_ref):
    length = x_ref.shape[0]
    real = len_ref[pl.program_id(0)]
    lane = lax.broadcasted_iota(jnp.int32, (1, PAIR), 1)
    valid = lax.broadcasted_iota(jnp.int32, (length, 1), 0) < real
    query = x_ref[:, 0:PAIR] * jnp.bfloat16(0.125)
    keys = x_ref[:, PAIR : 2 * PAIR]
    values_t = x_ref[:, 2 * PAIR : 3 * PAIR].T
    outs, logs = [], []
    for h in range(2):
        mine = (lane < DH) if h == 0 else (lane >= DH)
        q = jnp.where(mine, query, jnp.bfloat16(0))
        s = against(keys, q)
        s = jnp.where(valid, s, masked_score)
        top = jnp.max(s, axis=0, keepdims=True)
        e = jnp.exp(s - top)
        total = jnp.sum(e, axis=0, keepdims=True)
        p = (e * (1.0 / total)).astype(jnp.bfloat16)
        outs.append(plain(values_t[h * DH : (h + 1) * DH, :], p))
        logs.append(top + jnp.log(total))
    ctx_ref[...] = jnp.concatenate(outs, axis=0).T.astype(jnp.bfloat16)
    lse_ref[0, 0] = jnp.concatenate(logs, axis=0)


def attend(lengths, qkv, count):
    tokens, width = qkv.shape
    length = tokens // count
    pairs = width // (3 * PAIR)
    return pl.pallas_call(
        attend_kernel,
        grid=(count, pairs),
        in_specs=[
            pl.BlockSpec(memory_space=pltpu.SMEM),
            pl.BlockSpec((length, 3 * PAIR), lambda s, p: (s, p)),
        ],
        out_specs=[
            pl.BlockSpec((length, PAIR), lambda s, p: (s, p)),
            pl.BlockSpec((1, 1, 2, length), lambda s, p: (s, p, 0, 0)),
        ],
        out_shape=[
            jax.ShapeDtypeStruct((tokens, pairs * PAIR), jnp.bfloat16),
            jax.ShapeDtypeStruct((count, pairs, 2, length), jnp.float32),
        ],
        compiler_params=PARAMS,
        cost_estimate=pl.CostEstimate(
            flops=4 * tokens * length * 4 * pairs * PAIR, bytes_accessed=8 * tokens * width, transcendentals=0
        ),
    )(lengths, qkv)


def attend_back_kernel(len_ref, x_ref, lse_ref, dc_ref, out_ref):
    length = x_ref.shape[0]
    real = len_ref[pl.program_id(0)]
    lane = lax.broadcasted_iota(jnp.int32, (1, PAIR), 1)
    valid = lax.broadcasted_iota(jnp.int32, (length, 1), 0) < real
    query = x_ref[:, 0:PAIR] * jnp.bfloat16(0.125)
    keys = x_ref[:, PAIR : 2 * PAIR]
    keys_t = keys.T
    values = x_ref[:, 2 * PAIR : 3 * PAIR]
    d_ctx = dc_ref[...]
    dq, dk, dv = [], [], []
    for h in range(2):
        mine = (lane < DH) if h == 0 else (lane >= DH)
        q = jnp.where(mine, query, jnp.bfloat16(0))
        s = against(keys, q)
        s = jnp.where(valid, s, masked_score)
        p = jnp.exp(s - lse_ref[0, 0, h : h + 1, :])
        dv.append(plain(p.astype(jnp.bfloat16), d_ctx))
        dp = against(values, jnp.where(mine, d_ctx, jnp.bfloat16(0)))
        row = jnp.sum(p * dp, axis=0, keepdims=True)
        ds = (p * (dp - row)).astype(jnp.bfloat16)
        dk.append(plain(ds, query))
        dq.append(plain(keys_t[h * DH : (h + 1) * DH, :], ds))
    first = lane < DH
    out_ref[:, 0:PAIR] = (jnp.concatenate(dq, axis=0) * 0.125).T.astype(jnp.bfloat16)
    out_ref[:, PAIR : 2 * PAIR] = jnp.where(first, dk[0], dk[1]).astype(jnp.bfloat16)
    out_ref[:, 2 * PAIR : 3 * PAIR] = jnp.where(first, dv[0], dv[1]).astype(jnp.bfloat16)


def attend_back(lengths, qkv, lse, d_ctx, count):
    tokens, width = qkv.shape
    length = tokens // count
    pairs = width // (3 * PAIR)
    return pl.pallas_call(
        attend_back_kernel,
        grid=(count, pairs),
        in_specs=[
            pl.BlockSpec(memory_space=pltpu.SMEM),
            pl.BlockSpec((length, 3 * PAIR), lambda s, p: (s, p)),
            pl.BlockSpec((1, 1, 2, length), lambda s, p: (s, p, 0, 0)),
            pl.BlockSpec((length, PAIR), lambda s, p: (s, p)),
        ],
        out_specs=pl.BlockSpec((length, 3 * PAIR), lambda s, p: (s, p)),
        out_shape=jax.ShapeDtypeStruct((tokens, width), jnp.bfloat16),
        compiler_params=PARAMS,
        cost_estimate=pl.CostEstimate(
            flops=10 * tokens * length * 4 * pairs * PAIR, bytes_accessed=8 * tokens * width, transcendentals=0
        ),
    )(lengths, qkv, lse, d_ctx)


def by_pairs(q, k, v):
    rows = q.shape[0]
    pairs = q.shape[1] // PAIR
    parts = [a.reshape(rows, pairs, 1, PAIR) for a in (q, k, v)]
    return jnp.concatenate(parts, axis=2).reshape(rows, pairs * 3 * PAIR)


def per_device(
    inputs,
    lengths,
    w_query,
    b_query,
    w_key,
    w_value,
    b_value,
    w_output,
    b_output,
    gain_one,
    shift_one,
    w_up,
    b_up,
    w_down,
    b_down,
    gain_two,
    shift_two,
    cotangent,
    *,
    n,
):
    f32 = jnp.float32
    count, length, width = inputs.shape
    local = w_query.shape[1]
    flat = inputs.reshape(count * length, width)
    me = lax.axis_index("dp").astype(jnp.int32)
    bits = [1 << i for i in range(n.bit_length() - 1)]
    y_first = tuple(bits)
    z_first = (bits[0], bits[2], bits[1]) + tuple(bits[3:])

    wqkv = by_pairs(w_query, w_key, w_value)
    zero = jnp.zeros((local,), f32)
    bqkv = by_pairs(b_query.astype(f32)[None], zero[None], b_value.astype(f32)[None])
    biases = swap_x(jnp.concatenate([bqkv[0], b_up.astype(f32)])[None])
    bqkv_far, b_up_far = biases[:, : 3 * local], biases[:, 3 * local :]
    wqkv_far = fetch_other(wqkv, me, n, 2, 4)
    wo_far = fetch_other(w_output, me, n, 4, 2)
    wu_far = fetch_other(w_up, me, n, 2, 4)
    wd_far = fetch_other(w_down, me, n, 4, 2)

    gain_first = gain_one.astype(f32)
    gain_second = gain_two.astype(f32)

    qkv = (plain(flat, wqkv) + bqkv).astype(jnp.bfloat16)
    ctx, lse = attend(lengths, qkv, count)
    qkv_far = (plain(flat, wqkv_far) + bqkv_far).astype(jnp.bfloat16)
    ctx_far, lse_far = attend(lengths, qkv_far, count)
    attn = plain(ctx, w_output) + plain(ctx_far, wo_far)
    residual_one = flat.astype(f32) + attn + b_output.astype(f32)
    first, normed_one, inverse_one = norm_forward(residual_one, gain_first, shift_one.astype(f32))
    first_low = first.astype(jnp.bfloat16)
    act, slope = gelu_both(plain(first_low, w_up) + b_up.astype(f32))
    act_far, slope_far = gelu_both(plain(first_low, wu_far) + b_up_far)
    ffn = plain(act, w_down) + plain(act_far, wd_far)
    residual_two = first + ffn + b_down.astype(f32)
    final, normed_two, inverse_two = norm_forward(residual_two, gain_second, shift_two.astype(f32))
    layer_out = final.astype(jnp.bfloat16).reshape(count, length, width)

    tangent = cotangent.reshape(count * length, width).astype(f32)
    grad_gain_two = jnp.sum(tangent * normed_two, axis=0)
    grad_shift_two = jnp.sum(tangent, axis=0)
    d_second = norm_backward(tangent, normed_two, inverse_two, gain_second)
    d_ffn = d_second.astype(jnp.bfloat16)
    grad_b_down = jnp.sum(d_second, axis=0)
    sum_down = scatter_sum(plain(turned(d_ffn, me, n, y_first), act), n, y_first)
    d_pre = (against(d_ffn, w_down) * slope.astype(f32)).astype(jnp.bfloat16)
    grad_b_up = jnp.sum(d_pre.astype(f32), axis=0)
    sum_up = scatter_sum(plain(turned(first_low, me, n, y_first), d_pre), n, y_first)
    d_pre_far = (against(d_ffn, wd_far) * slope_far.astype(f32)).astype(jnp.bfloat16)
    d_first = d_second + against(d_pre, w_up) + against(d_pre_far, wu_far)
    grad_gain_one = jnp.sum(d_first * normed_one, axis=0)
    grad_shift_one = jnp.sum(d_first, axis=0)
    d_res_one = norm_backward(d_first, normed_one, inverse_one, gain_first)
    d_attn = d_res_one.astype(jnp.bfloat16)
    grad_b_output = jnp.sum(d_res_one, axis=0)
    sum_output = scatter_sum(plain(turned(d_attn, me, n, y_first), ctx), n, y_first)
    d_ctx = against(d_attn, w_output).astype(jnp.bfloat16)
    d_ctx_far = against(d_attn, wo_far).astype(jnp.bfloat16)
    d_qkv = attend_back(lengths, qkv, lse, d_ctx, count)
    grad_bqkv = jnp.sum(d_qkv.astype(f32), axis=0)
    sum_qkv = scatter_sum(plain(turned(flat, me, n, z_first), d_qkv), n, z_first)
    d_qkv_far = attend_back(lengths, qkv_far, lse_far, d_ctx_far, count)
    d_inputs = d_res_one + against(d_qkv, wqkv) + against(d_qkv_far, wqkv_far)
    grad_inputs = d_inputs.astype(jnp.bfloat16).reshape(count, length, width)

    vectors = jnp.concatenate(
        [
            grad_b_output,
            grad_gain_one,
            grad_shift_one,
            grad_b_down,
            grad_gain_two,
            grad_shift_two,
            grad_b_up,
            grad_bqkv,
        ]
    ).reshape(-1, 384)
    vectors = total_sum(vectors, n, y_first).reshape(-1)
    rows = width // n
    shared = lax.dynamic_slice_in_dim(vectors[: 6 * width].reshape(6, width), me * rows, rows, 1)
    hidden = b_up.shape[0]
    sum_b_up = vectors[6 * width : 6 * width + hidden]
    sum_bqkv = vectors[6 * width + hidden :].reshape(-1, 3, PAIR)
    split = sum_qkv.reshape(rows, -1, 3, PAIR)
    return (
        layer_out,
        grad_inputs,
        split[:, :, 0].reshape(rows, local),
        sum_bqkv[:, 0].reshape(local),
        split[:, :, 1].reshape(rows, local),
        split[:, :, 2].reshape(rows, local),
        sum_bqkv[:, 2].reshape(local),
        sum_output.T,
        shared[0],
        shared[1],
        shared[2],
        sum_up,
        sum_b_up,
        sum_down.T,
        shared[3],
        shared[4],
        shared[5],
    )


def solution(mesh):
    in_specs = (
        P("dp", None, None),
        P("dp"),
        P(None, "tensor"),
        P("tensor"),
        P(None, "tensor"),
        P(None, "tensor"),
        P("tensor"),
        P("tensor", None),
        P(),
        P(),
        P(),
        P(None, "tensor"),
        P("tensor"),
        P("tensor", None),
        P(),
        P(),
        P(),
        P("dp", None, None),
    )
    out_specs = (
        P("dp", None, None),
        P("dp", None, None),
        P("dp", "tensor"),
        P("tensor"),
        P("dp", "tensor"),
        P("dp", "tensor"),
        P("tensor"),
        P("tensor", "dp"),
        P("dp"),
        P("dp"),
        P("dp"),
        P("dp", "tensor"),
        P("tensor"),
        P("tensor", "dp"),
        P("dp"),
        P("dp"),
        P("dp"),
    )
    return jax.shard_map(
        functools.partial(per_device, n=mesh.shape["dp"]),
        mesh=mesh,
        in_specs=in_specs,
        out_specs=out_specs,
        check_vma=False,
    )
```

time: 918 us -> 365 us (0.40)
  waiting for transfers between devices: 639 us -> 110 us
  blocking collectives: 60.9 us -> 0 us
  Pallas kernels: 0 us -> 51.5 us
  starting transfers between devices: 1.3 us -> 41.6 us
  matrix products: 113 us -> 74.7 us
  between operations: 15.9 us -> 2.12 us
    psum x4 -> x0, waiting for transfers between devices: 256 us -> none  [the longest x1 88 us: per_device(): lax.psum(jnp.dot(context, w_output, preferred_element_type=jnp.float32),...]
    reduce_scatter x3 -> x0, waiting for transfers between devices: 199 us -> none  [the longest x1 79.4 us: per_device(): lax.psum_scatter(grad_w_up, 'dp', scatter_dimension=0, tiled=True)]
    unnamed x13 -> x0, waiting for transfers between devices: 184 us -> none
    ppermute x0 -> x53, waiting for transfers between devices: none -> 110 us  [the longest x48 104 us: swap_dp(): return lax.ppermute(value, 'dp', [(i, i ^ bit) for i in range(n)])]
    psum x1 -> x0, blocking collectives: 60.9 us -> none  [per_device(): lax.psum((grad_b_query, grad_b_value, grad_b_up), 'dp')]
    pallas_call x0 -> x12, Pallas kernels: none -> 51.5 us  [the longest x2 23.4 us: attend_back(): pl.pallas_call(attend_back_kernel, grid=(count, pairs), in_specs=[pl.Bloc...]
    dot_general x18 -> x12, matrix products: 93.7 us -> 43 us  [plain(): return jnp.dot(left, right, preferred_element_type=jnp.float32)]
    ppermute x0 -> x53, starting transfers between devices: none -> 41.6 us  [the longest x48 34.5 us: swap_dp(): return lax.ppermute(value, 'dp', [(i, i ^ bit) for i in range(n)])]
  transfers between devices with their start and end apart: 10 -> 53, of which waited for: 9 -> 17; matrix products, arithmetic and copies ran while one was open for 5% -> 23% of each run, Pallas kernels for 0% -> 10%
where the time goes in v1:
time: 365 us; the launch traced here: 360 us
  waiting for transfers between devices  110 us (30%)
  matrix products  74.7 us (20%)
  Pallas kernels  51.5 us (14%)
  local copies, waits for them, and re-layouts  46.5 us (13%)
  starting transfers between devices  41.6 us (11%)
  other arithmetic  33.9 us (9%)
    ppermute x48, waiting for transfers between devices, swap_dp(): return lax.ppermute(value, 'dp', [(i, i ^ bit) for i in range(n)])  104 us
    dot_general x12, matrix products, plain(): return jnp.dot(left, right, preferred_element_type=jnp.float32)  43 us
    ppermute x48, starting transfers between devices, swap_dp(): return lax.ppermute(value, 'dp', [(i, i ^ bit) for i in range(n)])  34.5 us
    dot_general x7, matrix products, against(): lax.dot_general(left, right, (((1,), (1,)), ((), ())), preferred_element_...  31.7 us
    unnamed x175, local copies, waits for them, and re-layouts  27.7 us
    pallas_call x2, Pallas kernels, attend_back(): pl.pallas_call(attend_back_kernel, grid=(count, pairs), in_specs=[pl.Bloc...  23.4 us
    pallas_call x2, Pallas kernels, attend(): pl.pallas_call(attend_kernel, grid=(count, pairs), in_specs=[pl.BlockSpec...  18.7 us
    add x14, other arithmetic, scatter_sum(): grad = grad[:half] + swap_dp(grad[half:], bit, n)  10.5 us
  transfers between devices with their start and end apart: 53, of which 17 were waited for; matrix products, arithmetic and copies ran while one was open for 23% of the time, Pallas kernels for 10%

profile of v1, /device:TPU:0, one launch (start us, length us, event | category | flops | bytes accessed | tf_op | source)
XLA Modules:
  0.0 360.0 jit_solution(18059320447193788760)
XLA Ops:
  15.8 5.1 %fusion.10.x_ref = bf16[1024,1152]{1,0:T(8,128)(2,1)} fusion(bf16[768,1152]{0,1:T(8,128)(2,1)} %bitcast.107, bf16[1024,768]{1,0:T(8,128)(2,1)S(1)} %bitcast.98, f32[1152]{0:T(1024)S(1)} %add.197), kind=kOutput, calls=%fused_computation.22 | convolution fusion | flops 1814298624 | bytes 5706240 | tf_op jit(solution)/shard_map/dot_general | solution.py:32
  21.0 5.3 %collective-permute-done.9.refs_0_ = f32[48,768]{1,0:T(8,128)S(1)} collective-permute-done((f32[48,768]{1,0:T(8,128)S(1)}, f32[48,768]{1,0:T(8,128)S(1)}, u32[]{:S(2)}, u32[]{:S(2)}) %collective-permute-start.9) | collective-permute-done | bytes 147488 | tf_op jit(solution)/shard_map/ppermute | solution.py:57
  39.8 9.5 %shard_map.305 = (bf16[1024,384]{1,0:T(8,128)(2,1)S(1)}, f32[2,3,2,512]{3,2,1,0:T(2,128)S(1)}) custom-call(s32[2]{0:T(128)S(1)} %copy-done.21, bf16[1024,1152]{1,0:T(8,128)(2,1)S(1)} %copy-done.23), custom_call_target="tpu_custom_call" | custom-call | flops 3221225472 | bytes 9437184 | tf_op jit(solution)/shard_map/pallas_call | solution.py:166
  63.8 8.6 %collective-permute-done.3.refs_3_ = f32[96,1152]{1,0:T(8,128)} collective-permute-done((f32[96,1152]{1,0:T(8,128)}, f32[96,1152]{1,0:T(8,128)}, u32[]{:S(2)}, u32[]{:S(2)}) %collective-permute-start.3) | collective-permute-done | bytes 442400 | tf_op jit(solution)/shard_map/ppermute | solution.py:61
  82.8 9.3 %shard_map.307 = (bf16[1024,384]{1,0:T(8,128)(2,1)S(1)}, f32[2,3,2,512]{3,2,1,0:T(2,128)S(1)}) custom-call(s32[2]{0:T(128)S(1)} %copy-done.21, bf16[1024,1152]{1,0:T(8,128)(2,1)S(1)} %fusion.11.x_ref), custom_call_target="tpu_custom_call" | custom-call | flops 3221225472 | bytes 9437184 | tf_op jit(solution)/shard_map/pallas_call | solution.py:166
  96.6 7.9 %collective-permute-done.19.refs_2_ = f32[96,1536]{1,0:T(8,128)S(1)} collective-permute-done((f32[96,1536]{1,0:T(8,128)S(1)}, f32[96,1536]{1,0:T(8,128)S(1)}, u32[]{:S(2)}, u32[]{:S(2)}) %collective-permute-start.19) | collective-permute-done | bytes 589856 | tf_op jit(solution)/shard_map/ppermute | solution.py:61
  104.5 5.2 %multiply_convert_fusion.3 = (bf16[1024,1536]{1,0:T(8,128)(2,1)S(1)}, f32[1024,1536]{1,0:T(8,128)}) fusion(f32[1536]{0:T(1024)S(1)} %copy-done.55, bf16[1024,768]{1,0:T(8,128)(2,1)S(1)} %fusion.21.x_ref, bf16[768,1536]{1,0:T(8,128)(2,1)S(1)} %copy-done.52), kind=kOutput, calls=%fused_computation.17 | convolution fusion | flops 2425356288 | bytes 13375488 | tf_op jit(solution)/shard_map/dot_general | solution.py:32
  110.8 6.0 %collective-permute-done.20.refs_3_ = f32[96,1536]{1,0:T(8,128)S(1)} collective-permute-done((f32[96,1536]{1,0:T(8,128)}, f32[96,1536]{1,0:T(8,128)S(1)}, u32[]{:S(2)}, u32[]{:S(2)}) %collective-permute-start.20) | collective-permute-done | bytes 589856 | tf_op jit(solution)/shard_map/ppermute | solution.py:61
  117.4 4.3 %fusion.35 = f32[1024,768]{1,0:T(8,128)} fusion(bf16[1024,1536]{1,0:T(8,128)(2,1)S(1)} %get-tuple-element.51, bf16[1536,768]{1,0:T(8,128)(2,1)S(1)} %copy-done.51), kind=kOutput, calls=%fused_computation.121 | convolution fusion | flops 2415919104 | bytes 8650752 | tf_op jit(solution)/shard_map/dot_general | solution.py:32
  126.2 6.1 %fusion.36 = f32[1024,1536]{1,0:T(8,128)} fusion(bf16[1024,768]{1,0:T(8,128)(2,1)S(1)} %fusion.21.x_ref, bf16[768,1536]{1,0:T(8,128)(2,1)} %shard_map.309), kind=kOutput, calls=%fused_computation.122 | convolution fusion | flops 2415919104 | bytes 10223616 | tf_op jit(solution)/shard_map/dot_general | solution.py:32
  135.0 7.0 %fusion.30 = (f32[1024]{0:T(1024)S(1)}, f32[1024,768]{1,0:T(8,128)S(1)}) fusion(f32[768]{0:T(1024)S(1)} %copy-done.64, f32[1024,768]{1,0:T(8,128)} %fusion.35, bf16[1536,768]{1,0:T(8,128)(2,1)} %shard_map.310, f32[1024,1536]{1,0:T(8,128)} %fusion.36, f32[1536]{0:T(1024)S(1)} %slice_reduce_fusion.3, f32[768]{0:T(1024)S(1)} %copy-done.59, ...), kind=kOutput, calls=%fused_computation.117 | convolution fusion | flops 2431646720 | bytes 18115584 | tf_op jit(solution)/shard_map/dot_general | solution.py:32
  147.0 4.7 %convert_reduce_fusion = (f32[1536]{0:T(1024)S(1)}, bf16[1024,1536]{1,0:T(8,128)(2,1)S(1)}) fusion(f32[1024,1536]{1,0:T(8,128)S(1)} %bitcast.124, f32[1536]{0:T(1024)S(1)} %copy-done.55, bf16[1536,768]{1,0:T(8,128)(2,1)S(1)} %copy-done.51, f32[1024,768]{1,0:T(8,128)S(1)} %get-tuple-element.39), kind=kOutput, calls=%fused_computation.12 | convolution fusion | flops 2440296960 | bytes 14954496 | tf_op jit(solution)/shard_map/dot_general | solution.py:26
  153.5 4.3 %fusion.37 = f32[1024,768]{1,0:T(8,128)} fusion(bf16[1024,1536]{1,0:T(8,128)(2,1)S(1)} %get-tuple-element.57, bf16[768,1536]{1,0:T(8,128)(2,1)S(1)} %copy-done.53), kind=kOutput, calls=%fused_computation.123 | convolution fusion | flops 2415919104 | bytes 8650752 | tf_op jit(solution)/shard_map/dot_general | solution.py:26
  157.8 14.2 %multiply_reduce_fusion = (f32[768]{0:T(1024)S(1)}, f32[1024]{0:T(1024)S(1)}, f32[1024]{0:T(1024)S(1)}, f32[768]{0:T(1024)S(1)}, f32[1024,768]{1,0:T(8,128)}) fusion(f32[1024,768]{1,0:T(8,128)} %copy-done.31, f32[1024]{0:T(1024)S(1)} %add_rsqrt_fusion.1, f32[1024]{0:T(1024)S(1)} %broadcast_multiply_fusion.4, f32[768]{0:T(1024)S(1)} %convert_element_type.119, ...), kind=kOutput, calls=%fused_computation.36 | convolution fusion | flops 4861718528 | bytes 23624704 | tf_op jit(solution)/shard_map/dot_general | solution.py:26
  182.1 11.7 %shard_map.311 = bf16[1024,1152]{1,0:T(8,128)(2,1)S(1)} custom-call(s32[2]{0:T(128)S(1)} %copy-done.21, bf16[1024,1152]{1,0:T(8,128)(2,1)S(1)} %copy-done.24, f32[2,3,2,512]{3,2,1,0:T(2,128)S(1)} %copy-done.28, bf16[1024,384]{1,0:T(8,128)(2,1)S(1)} %convolution_convert_fusion.1.dc_ref), custom_call_target="tpu_custom_call" | custom-call | flops 8053063680 | bytes 9437184 | tf_op jit(solution)/shard_map/pallas_call | solution.py:221
  217.1 11.7 %shard_map.312 = bf16[1024,1152]{1,0:T(8,128)(2,1)S(1)} custom-call(s32[2]{0:T(128)S(1)} %copy-done.21, bf16[1024,1152]{1,0:T(8,128)(2,1)S(1)} %copy-done.26, f32[2,3,2,512]{3,2,1,0:T(2,128)S(1)} %copy-done.30, bf16[1024,384]{1,0:T(8,128)(2,1)S(1)} %copy-done.22), custom_call_target="tpu_custom_call" | custom-call | flops 8053063680 | bytes 9437184 | tf_op jit(solution)/shard_map/pallas_call | solution.py:221
  248.1 5.9 %collective-permute-done.42 = f32[192,384]{1,0:T(8,128)S(1)} collective-permute-done((f32[192,384]{1,0:T(8,128)S(1)}, f32[192,384]{1,0:T(8,128)S(1)}, u32[]{:S(2)}, u32[]{:S(2)}) %collective-permute-start.42) | collective-permute-done | bytes 294944 | tf_op jit(solution)/shard_map/ppermute | solution.py:61
  265.1 14.7 %collective-permute-done.34 = f32[192,1152]{1,0:T(8,128)S(1)} collective-permute-done((f32[192,1152]{1,0:T(8,128)S(1)}, f32[192,1152]{1,0:T(8,128)S(1)}, u32[]{:S(2)}, u32[]{:S(2)}) %collective-permute-start.34) | collective-permute-done | bytes 884768 | tf_op jit(solution)/shard_map/ppermute | solution.py:61
  286.6 16.5 %collective-permute-done.35 = f32[96,1152]{1,0:T(8,128)S(1)} collective-permute-done((f32[96,1152]{1,0:T(8,128)S(1)}, f32[96,1152]{1,0:T(8,128)S(1)}, u32[]{:S(2)}, u32[]{:S(2)}) %collective-permute-start.35) | collective-permute-done | bytes 442400 | tf_op jit(solution)/shard_map/ppermute | solution.py:61
  306.7 5.2 %collective-permute-done.36 = f32[48,1152]{1,0:T(8,128)S(1)} collective-permute-done((f32[48,1152]{1,0:T(8,128)S(1)}, f32[48,1152]{1,0:T(8,128)S(1)}, u32[]{:S(2)}, u32[]{:S(2)}) %collective-permute-start.36) | collective-permute-done | bytes 221216 | tf_op jit(solution)/shard_map/ppermute | solution.py:61
  317.9 5.3 %collective-permute-done.50 = f32[192,1536]{1,0:T(8,128)} collective-permute-done((f32[192,1536]{1,0:T(8,128)}, f32[192,1536]{1,0:T(8,128)}, u32[]{:S(2)}, u32[]{:S(2)}) %collective-permute-start.50) | collective-permute-done | bytes 1179680 | tf_op jit(solution)/shard_map/ppermute | solution.py:61
  328.7 3.7 %collective-permute-done.47 = f32[96,1536]{1,0:T(8,128)S(1)} collective-permute-done((f32[96,1536]{1,0:T(8,128)S(1)}, f32[96,1536]{1,0:T(8,128)S(1)}, u32[]{:S(2)}, u32[]{:S(2)}) %collective-permute-start.47) | collective-permute-done | bytes 589856 | tf_op jit(solution)/shard_map/ppermute | solution.py:61
  332.6 12.1 %collective-permute-done.51 = f32[96,1536]{1,0:T(8,128)S(1)} collective-permute-done((f32[96,1536]{1,0:T(8,128)S(1)}, f32[96,1536]{1,0:T(8,128)S(1)}, u32[]{:S(2)}, u32[]{:S(2)}) %collective-permute-start.51) | collective-permute-done | bytes 589856 | tf_op jit(solution)/shard_map/ppermute | solution.py:61
  346.2 12.7 %collective-permute-done.52 = f32[48,1536]{1,0:T(8,128)S(1)} collective-permute-done((f32[48,1536]{1,0:T(8,128)S(1)}, f32[48,1536]{1,0:T(8,128)S(1)}, u32[]{:S(2)}, u32[]{:S(2)}) %collective-permute-start.52) | collective-permute-done | bytes 294944 | tf_op jit(solution)/shard_map/ppermute | solution.py:61
  (381 shorter events, 160.6 us)
Async XLA Ops:
  9.6 20.1 %collective-permute-start = (f32[96,1152]{1,0:T(8,128)}, f32[96,1152]{1,0:T(8,128)}, u32[]{:S(2)}, u32[]{:S(2)}) collective-permute-start(f32[96,1152]{1,0:T(8,128)} %convert_element_type.113), channel_id=1, source_target_pairs={{0,1},{1,0},{2,3},{3,2},{4,5},{5,4},{6,7},{7,6},{8,9},{9,8},{10,11... | collective-permute-start | bytes 1327112 | tf_op jit(solution)/shard_map/ppermute | solution.py:57
  12.8 19.2 %collective-permute-start.8 = (f32[1,2688]{1,0:T(1,128)S(1)}, f32[1,2688]{1,0:T(1,128)S(1)}, u32[]{:S(2)}, u32[]{:S(2)}) collective-permute-start(f32[1,2688]{1,0:T(1,128)S(1)} %broadcast_in_dim.2), channel_id=1, source_target_pairs={{0,1},{1,0},{2,3},{3,2},{4,5},{5,4},{6,7},{7,6},{8,9},{9,8},{10,11... | collective-permute-start | bytes 32264 | tf_op jit(solution)/shard_map/ppermute | solution.py:57
  29.6 21.3 %collective-permute-start.1 = (f32[96,1152]{1,0:T(8,128)}, f32[96,1152]{1,0:T(8,128)}, u32[]{:S(2)}, u32[]{:S(2)}) collective-permute-start(f32[96,1152]{1,0:T(8,128)} %collective-permute-done.refs_0_), channel_id=1, source_target_pairs={{0,4},{2,6},{4,0},{6,2},{8,12},{10,14},{12,8},{14,10},{16,20},{18,... | collective-permute-start | bytes 1327112 | tf_op jit(solution)/shard_map/ppermute | solution.py:61
  32.0 22.4 %collective-permute-start.17 = (f32[96,1536]{1,0:T(8,128)}, f32[96,1536]{1,0:T(8,128)S(1)}, u32[]{:S(2)}, u32[]{:S(2)}) collective-permute-start(f32[96,1536]{1,0:T(8,128)} %dynamic-slice_convert_fusion.1), channel_id=1, source_target_pairs={{0,1},{1,0},{2,3},{3,2},{4,5},{5,4},{6,7},{7,6},{8,9},{9,8},{10,11... | collective-permute-start | bytes 1769480 | tf_op jit(solution)/shard_map/ppermute | solution.py:57
  35.3 27.5 %collective-permute-start.25 = (f32[192,768]{1,0:T(8,128)}, f32[192,768]{1,0:T(8,128)S(1)}, u32[]{:S(2)}, u32[]{:S(2)}) collective-permute-start(f32[192,768]{1,0:T(8,128)} %dynamic-slice_convert_fusion), channel_id=1, source_target_pairs={{0,1},{1,0},{2,3},{3,2},{4,5},{5,4},{6,7},{7,6},{8,9},{9,8},{10,11... | collective-permute-start | bytes 1769480 | tf_op jit(solution)/shard_map/ppermute | solution.py:57
  50.9 21.5 %collective-permute-start.3 = (f32[96,1152]{1,0:T(8,128)}, f32[96,1152]{1,0:T(8,128)}, u32[]{:S(2)}, u32[]{:S(2)}) collective-permute-start(f32[96,1152]{1,0:T(8,128)} %collective-permute-done.1.refs_1_), channel_id=1, source_target_pairs={{0,8},{2,10},{4,12},{6,14},{8,0},{10,2},{12,4},{14,6},{16,24},{18,... | collective-permute-start | bytes 1327112 | tf_op jit(solution)/shard_map/ppermute | solution.py:61
  54.4 21.8 %collective-permute-start.18 = (f32[96,1536]{1,0:T(8,128)S(1)}, f32[96,1536]{1,0:T(8,128)}, u32[]{:S(2)}, u32[]{:S(2)}) collective-permute-start(f32[96,1536]{1,0:T(8,128)S(1)} %collective-permute-done.17.refs_0_), channel_id=1, source_target_pairs={{0,4},{2,6},{4,0},{6,2},{8,12},{10,14},{12,8},{14,10},{16,20},{18,... | collective-permute-start | bytes 1769480 | tf_op jit(solution)/shard_map/ppermute | solution.py:61
  75.7 19.4 %collective-permute-start.26 = (f32[192,768]{1,0:T(8,128)S(1)}, f32[192,768]{1,0:T(8,128)S(1)}, u32[]{:S(2)}, u32[]{:S(2)}) collective-permute-start(f32[192,768]{1,0:T(8,128)S(1)} %collective-permute-done.25.refs_0_), channel_id=1, source_target_pairs={{0,8},{2,10},{4,12},{6,14},{8,0},{10,2},{12,4},{14,6},{16,24},{18,... | collective-permute-start | bytes 1769480 | tf_op jit(solution)/shard_map/ppermute | solution.py:61
  76.9 27.7 %collective-permute-start.19 = (f32[96,1536]{1,0:T(8,128)S(1)}, f32[96,1536]{1,0:T(8,128)S(1)}, u32[]{:S(2)}, u32[]{:S(2)}) collective-permute-start(f32[96,1536]{1,0:T(8,128)S(1)} %collective-permute-done.17.refs_0_), channel_id=1, source_target_pairs={{0,8},{2,10},{4,12},{6,14},{8,0},{10,2},{12,4},{14,6},{16,24},{18,... | collective-permute-start | bytes 1769480 | tf_op jit(solution)/shard_map/ppermute | solution.py:61
  78.4 31.4 %collective-permute-start.21 = (f32[96,1536]{1,0:T(8,128)S(1)}, f32[96,1536]{1,0:T(8,128)S(1)}, u32[]{:S(2)}, u32[]{:S(2)}) collective-permute-start(f32[96,1536]{1,0:T(8,128)S(1)} %collective-permute-done.17.refs_0_), channel_id=1, source_target_pairs={{0,2},{2,0},{4,6},{6,4},{8,10},{10,8},{12,14},{14,12},{16,18},{18,... | collective-permute-start | bytes 1769480 | tf_op jit(solution)/shard_map/ppermute | solution.py:61
  78.5 38.3 %collective-permute-start.20 = (f32[96,1536]{1,0:T(8,128)}, f32[96,1536]{1,0:T(8,128)S(1)}, u32[]{:S(2)}, u32[]{:S(2)}) collective-permute-start(f32[96,1536]{1,0:T(8,128)} %collective-permute-done.18.refs_1_), channel_id=1, source_target_pairs={{0,8},{2,10},{4,12},{6,14},{8,0},{10,2},{12,4},{14,6},{16,24},{18,... | collective-permute-start | bytes 1769480 | tf_op jit(solution)/shard_map/ppermute | solution.py:61
  95.1 21.7 %collective-permute-start.22 = (f32[96,1536]{1,0:T(8,128)}, f32[96,1536]{1,0:T(8,128)S(1)}, u32[]{:S(2)}, u32[]{:S(2)}) collective-permute-start(f32[96,1536]{1,0:T(8,128)} %collective-permute-done.18.refs_1_), channel_id=1, source_target_pairs={{0,2},{2,0},{4,6},{6,4},{8,10},{10,8},{12,14},{14,12},{16,18},{18,... | collective-permute-start | bytes 1769480 | tf_op jit(solution)/shard_map/ppermute | solution.py:61
  109.8 22.4 %collective-permute-start.29 = (f32[192,768]{1,0:T(8,128)S(1)}, f32[192,768]{1,0:T(8,128)S(1)}, u32[]{:S(2)}, u32[]{:S(2)}) collective-permute-start(f32[192,768]{1,0:T(8,128)S(1)} %collective-permute-done.25.refs_0_), channel_id=1, source_target_pairs={{0,2},{2,0},{4,6},{6,4},{8,10},{10,8},{12,14},{14,12},{16,18},{18,... | collective-permute-start | bytes 1769480 | tf_op jit(solution)/shard_map/ppermute | solution.py:61
  110.8 21.4 %collective-permute-start.30 = (f32[192,768]{1,0:T(8,128)S(1)}, f32[192,768]{1,0:T(8,128)S(1)}, u32[]{:S(2)}, u32[]{:S(2)}) collective-permute-start(f32[192,768]{1,0:T(8,128)S(1)} %collective-permute-done.26.refs_1_), channel_id=1, source_target_pairs={{0,2},{2,0},{4,6},{6,4},{8,10},{10,8},{12,14},{14,12},{16,18},{18,... | collective-permute-start | bytes 1769480 | tf_op jit(solution)/shard_map/ppermute | solution.py:61
  198.7 56.7 %collective-permute-start.33 = (f32[384,1152]{1,0:T(8,128)}, f32[384,1152]{1,0:T(8,128)}, u32[]{:S(2)}, u32[]{:S(2)}) collective-permute-start(f32[384,1152]{1,0:T(8,128)} %slice.201), channel_id=1, source_target_pairs={{0,2},{2,0},{4,6},{6,4},{8,10},{10,8},{12,14},{14,12},{16,18},{18,... | collective-permute-start | bytes 5308424 | tf_op jit(solution)/shard_map/ppermute | solution.py:61
  203.0 41.8 %collective-permute-start.41 = (f32[384,384]{1,0:T(8,128)}, f32[384,384]{1,0:T(8,128)}, u32[]{:S(2)}, u32[]{:S(2)}) collective-permute-start(f32[384,384]{1,0:T(8,128)} %slice.215), channel_id=1, source_target_pairs={{0,2},{2,0},{4,6},{6,4},{8,10},{10,8},{12,14},{14,12},{16,18},{18,... | collective-permute-start | bytes 1769480 | tf_op jit(solution)/shard_map/ppermute | solution.py:61
  209.5 51.8 %collective-permute-start.45 = (f32[384,1536]{1,0:T(8,128)}, f32[384,1536]{1,0:T(8,128)}, u32[]{:S(2)}, u32[]{:S(2)}) collective-permute-start(f32[384,1536]{1,0:T(8,128)} %slice.224), channel_id=1, source_target_pairs={{0,2},{2,0},{4,6},{6,4},{8,10},{10,8},{12,14},{14,12},{16,18},{18,... | collective-permute-start | bytes 7077896 | tf_op jit(solution)/shard_map/ppermute | solution.py:61
  214.5 66.1 %collective-permute-start.49 = (f32[384,1536]{1,0:T(8,128)}, f32[384,1536]{1,0:T(8,128)}, u32[]{:S(2)}, u32[]{:S(2)}) collective-permute-start(f32[384,1536]{1,0:T(8,128)} %slice.233), channel_id=1, source_target_pairs={{0,2},{2,0},{4,6},{6,4},{8,10},{10,8},{12,14},{14,12},{16,18},{18,... | collective-permute-start | bytes 7077896 | tf_op jit(solution)/shard_map/ppermute | solution.py:61
  257.2 22.6 %collective-permute-start.34 = (f32[192,1152]{1,0:T(8,128)S(1)}, f32[192,1152]{1,0:T(8,128)S(1)}, u32[]{:S(2)}, u32[]{:S(2)}) collective-permute-start(f32[192,1152]{1,0:T(8,128)S(1)} %slice.203), channel_id=1, source_target_pairs={{0,8},{2,10},{4,12},{6,14},{8,0},{10,2},{12,4},{14,6},{16,24},{18,... | collective-permute-start | bytes 2654216 | tf_op jit(solution)/shard_map/ppermute | solution.py:61
  261.1 45.0 %collective-permute-start.44 = (f32[48,384]{1,0:T(8,128)S(1)}, f32[48,384]{1,0:T(8,128)S(1)}, u32[]{:S(2)}, u32[]{:S(2)}) collective-permute-start(f32[48,384]{1,0:T(8,128)S(1)} %slice.221), channel_id=1, source_target_pairs={{0,16},{2,18},{4,20},{6,22},{8,24},{10,26},{12,28},{14,30},{16,0},... | collective-permute-start | bytes 221192 | tf_op jit(solution)/shard_map/ppermute | solution.py:61
  264.5 49.9 %collective-permute-start.46 = (f32[192,1536]{1,0:T(8,128)}, f32[192,1536]{1,0:T(8,128)S(1)}, u32[]{:S(2)}, u32[]{:S(2)}) collective-permute-start(f32[192,1536]{1,0:T(8,128)} %slice.226), channel_id=1, source_target_pairs={{0,4},{2,6},{4,0},{6,2},{8,12},{10,14},{12,8},{14,10},{16,20},{18,... | collective-permute-start | bytes 3538952 | tf_op jit(solution)/shard_map/ppermute | solution.py:61
  280.0 23.2 %collective-permute-start.35 = (f32[96,1152]{1,0:T(8,128)S(1)}, f32[96,1152]{1,0:T(8,128)S(1)}, u32[]{:S(2)}, u32[]{:S(2)}) collective-permute-start(f32[96,1152]{1,0:T(8,128)S(1)} %slice.205), channel_id=1, source_target_pairs={{0,4},{2,6},{4,0},{6,2},{8,12},{10,14},{12,8},{14,10},{16,20},{18,... | collective-permute-start | bytes 1327112 | tf_op jit(solution)/shard_map/ppermute | solution.py:61
  285.2 37.9 %collective-permute-start.50 = (f32[192,1536]{1,0:T(8,128)}, f32[192,1536]{1,0:T(8,128)}, u32[]{:S(2)}, u32[]{:S(2)}) collective-permute-start(f32[192,1536]{1,0:T(8,128)} %slice.235), channel_id=1, source_target_pairs={{0,4},{2,6},{4,0},{6,2},{8,12},{10,14},{12,8},{14,10},{16,20},{18,... | collective-permute-start | bytes 3538952 | tf_op jit(solution)/shard_map/ppermute | solution.py:61
  324.6 20.1 %collective-permute-start.51 = (f32[96,1536]{1,0:T(8,128)S(1)}, f32[96,1536]{1,0:T(8,128)S(1)}, u32[]{:S(2)}, u32[]{:S(2)}) collective-permute-start(f32[96,1536]{1,0:T(8,128)S(1)} %slice.237), channel_id=1, source_target_pairs={{0,8},{2,10},{4,12},{6,14},{8,0},{10,2},{12,4},{14,6},{16,24},{18,... | collective-permute-start | bytes 1769480 | tf_op jit(solution)/shard_map/ppermute | solution.py:61
  (109 other events, 917.2 us)
